TPU v7x, 128 devices: a whole 4x4x4 slice. The times are simulated.
128 devices in a mesh: row: 16 (over y_lo, z, core), col: 8 (over y_hi, x).
Axes of the slice: x: 4, y: 4 (y_hi: 2, y_lo: 2; y = y_hi * 2 + y_lo), z: 4, core: 2. Of those that a mesh axis runs over, the one named last changes fastest.
Arguments:
- features: bfloat16 [65536, 512], P(('row', 'col')), may hold values from -6 to 6
- partition_of: int32 [65536], P(('row', 'col')), may hold values from 0 to 127, as said below
- weight: bfloat16 [512, 512], replicated, may hold values from -0.25 to 0.25
- tile_values: bfloat16 [16, 8, 192, 128, 128], P('row', 'col'), may hold values from -0.109375 to 0.109375
- tile_rows: int32 [16, 8, 192], P('row', 'col'), may hold values from 0 to 31
- tile_cols: int32 [16, 8, 192], P('row', 'col'), may hold values from 0 to 63
- tile_count: int32 [16, 8], P('row', 'col'), may hold values from 48 to 192, as said below
- out_cotangent: bfloat16 [65536, 512], P('row'), may hold values from -6 to 6
Outputs:
- activations: bfloat16 [65536, 512], P(('row', 'col'))
- weight_grad: float32 [512, 512], replicated
Inputs may be any that keep to these rules, and one draw needn't show every extreme that they name: `partition_of`: of the 512 regions of each device in detection order, exactly 4 go to each partition. `tile_count`: some grid position has all 192 slots live in every draw.
All inputs are finite; a program needn't handle non-finite values.
Results may differ from a plain program's by a relative error of at most 0.005.
Values may be sent and summed in bfloat16 or wider, within the bound.
No kernel may reach another device: no remote copies, remote signals or barrier semaphores. Data moves between devices by JAX's collectives and lax.ppermute only.
A program may use at most 192 MiB of HBM per device.

v0:
```python
import math
import jax
import jax.numpy as jnp
from jax import lax
from jax.sharding import PartitionSpec as P


def silu_slope(pre):
    sigmoid = jax.nn.sigmoid(pre)
    return sigmoid * (1.0 + pre * (1.0 - sigmoid))


def regroup(features, partition_of, n_row, n_col):
    slots, feature_width = features.shape
    per_peer = slots // (n_row * n_col)
    ordering = jnp.argsort(partition_of, stable=True)
    outgoing = features[ordering]
    shaped = outgoing.reshape(n_row * n_col, per_peer, feature_width)
    arrived = lax.all_to_all(shaped, ("row", "col"), split_axis=0, concat_axis=0, tiled=True)
    return arrived.reshape(slots, feature_width)


def tile_products(blocks, row_index, column_index, live_count, sources, out_tiles, forward):
    tile_size = blocks.shape[-1]
    feature_width = sources.shape[-1]
    source_tiles = sources.reshape(-1, tile_size, feature_width)
    empty = jnp.zeros((out_tiles, tile_size, feature_width), jnp.float32)
    block_total = (live_count + 31) // 32

    def one_block(block_step, totals):
        first_slot = block_step * 32
        tile_block = lax.dynamic_slice_in_dim(blocks, first_slot, 32, 0)
        row_part = lax.dynamic_slice_in_dim(row_index, first_slot, 32, 0)
        column_part = lax.dynamic_slice_in_dim(column_index, first_slot, 32, 0)
        is_live = first_slot + jnp.arange(32, dtype=jnp.int32) < live_count
        tile_block = jnp.where(is_live[:, None, None], tile_block, jnp.zeros_like(tile_block))
        if forward:
            picked = source_tiles[column_part]
            products = jnp.einsum(
                "tij,tjf->tif", tile_block, picked, preferred_element_type=jnp.float32
            )
            return totals.at[row_part].add(products)
        picked = source_tiles[row_part]
        products = jnp.einsum(
            "tij,tif->tjf", tile_block, picked, preferred_element_type=jnp.float32
        )
        return totals.at[column_part].add(products)

    totals = lax.fori_loop(0, block_total, one_block, empty)
    return totals.reshape(out_tiles * tile_size, feature_width)


def shards(
    features, partition_of, weight, tile_values, tile_rows, tile_cols, tile_count, out_cotangent
):
    n_row = lax.axis_size("row")
    n_col = lax.axis_size("col")
    regrouped = regroup(features, partition_of, n_row, n_col)
    slots, feature_width = regrouped.shape
    tile_size = tile_values.shape[-1]
    blocks = tile_values.reshape(-1, tile_size, tile_size)
    row_index = tile_rows.reshape(-1)
    column_index = tile_cols.reshape(-1)
    live_count = tile_count.reshape(())
    row_tiles = slots * n_col // tile_size
    column_tiles = slots * n_row // tile_size
    hidden = jnp.dot(regrouped, weight, preferred_element_type=jnp.float32).astype(jnp.bfloat16)
    hidden_columns = lax.all_gather(hidden, "row", axis=0, tiled=True)
    partial_value = tile_products(
        blocks, row_index, column_index, live_count, hidden_columns, row_tiles, True
    )
    position = lax.axis_index("col") * slots
    pre = lax.psum(partial_value, "col")
    own_pre = lax.dynamic_slice_in_dim(pre, position, slots, 0)
    activations = jax.nn.silu(own_pre).astype(jnp.bfloat16)
    slope = (out_cotangent.astype(jnp.float32) * silu_slope(pre)).astype(jnp.bfloat16)
    back_partial = tile_products(
        blocks, row_index, column_index, live_count, slope, column_tiles, False
    )
    hidden_grad = lax.psum_scatter(back_partial, "row", scatter_dimension=0, tiled=True)
    local_grad = jnp.dot(
        regrouped.astype(jnp.float32).T,
        hidden_grad,
        precision=lax.Precision.HIGHEST,
        preferred_element_type=jnp.float32,
    )
    weight_grad = lax.psum(local_grad, ("row", "col")) * (1.0 / math.sqrt(slots * n_row * n_col))
    return (activations, weight_grad)


def solution(mesh):
    placed = (
        P(("row", "col"), None),
        P(("row", "col")),
        P(),
        P("row", "col", None, None, None),
        P("row", "col", None),
        P("row", "col", None),
        P("row", "col"),
        P("row", None),
    )
    return jax.shard_map(
        shards,
        mesh=mesh,
        in_specs=placed,
        out_specs=(P(("row", "col"), None), P()),
        check_vma=False,
    )
```

profile of v0, /device:TPU:1, one launch (start us, length us, event | category | flops | bytes accessed | tf_op | source)
XLA Modules:
  0.0 937.0 jit_solution(18352285362092890931)
XLA Ops:
  7.2 0.0 copy-start
  7.2 0.0 all-gather.2.cloned.1.call-start
  7.2 4.5 sort.17
  11.7 0.0 copy-done
  11.7 0.0 copy-start.4
  11.8 0.0 copy-start.5
  11.8 2.0 gather_fusion.2
  13.8 0.1 reshape.48
  13.9 23.8 %all_to_all.5 = bf16[128,4,512]{2,1,0:T(4,128)(2,1)S(1)} all-to-all(bf16[128,4,512]{2,1,0:T(4,128)(2,1)S(1)} %reshape.48), channel_id=1, replica_groups=mesh['row'=16,'col'=8] {'row','col'}, dimensions={0} | all-to-all | bytes 1048576 | tf_op jit(solution)/shard_map/all_to_all | solution.py:19
  37.7 0.1 reshape.49
  37.9 0.0 copy-start.2
  37.9 2.5 convolution_convert_fusion
  40.3 0.0 all-gather.2.cloned.1.call-update
  40.4 0.0 all-reduce.3.cloned.1.call-start
  41.1 49.4 %all-gather.2.cloned.1.call-done = bf16[8192,512]{1,0:T(8,128)(2,1)} async-done(((bf16[512,512]{1,0:T(8,128)(2,1)}), bf16[8192,512]{1,0:T(8,128)(2,1)}) %all-gather.2.cloned.1.call-update) | async-done | bytes 8388624 | tf_op jit(solution)/shard_map/all_gather | solution.py:68
  90.5 4.3 broadcast_in_dim.36
  94.8 0.0 copy-done.4
  94.8 0.0 copy-done.5
  94.8 97.0 %while.20 = (s32[]{:T(128)}, f32[32,128,512]{2,1,0:T(8,128)}, s32[]{:T(128)}, s32[192]{0:T(256)S(1)}, s32[]{:T(128)}, /*index=5*/bf16[192,128,128]{2,1,0:T(8,128...) while((s32[]{:T(128)}, f32[32,128,512]{2,1,0:T(8,128)}, ...), condition=%wide.region_3.4_spmd, body=%wide.region_1.3_spmd.sunk | while | flops 539493632 | bytes 47191152 | solution.py:49
  94.8 0.7 add_compare_fusion.4
  95.5 0.1 compare_select_fusion.7
  95.6 6.1 gather_fusion
  101.7 7.0 fusion.29
  108.7 18.8 %scatter_fusion = f32[32,128,512]{2,1,0:T(8,128)} fusion(f32[32,128,512]{2,1,0:T(8,128)} %get-tuple-element.257, s32[32]{0:T(128)S(1)} %get-tuple-element.232, f32[32,128,512]{2,1,0:T(8,128)} %fusion.29), kind=kCustom, calls=%fused_computation.3.clone.1 | custom fusion | flops 2097152 | bytes 25165952 | tf_op jit(solution)/shard_map/while/body/scatter-add | solution.py:42
  127.5 0.7 add_compare_fusion.4
  128.2 0.1 compare_select_fusion.7
  128.3 6.1 gather_fusion
  134.4 7.0 fusion.29
  141.4 18.5 %scatter_fusion = f32[32,128,512]{2,1,0:T(8,128)} fusion(f32[32,128,512]{2,1,0:T(8,128)} %get-tuple-element.257, s32[32]{0:T(128)S(1)} %get-tuple-element.232, f32[32,128,512]{2,1,0:T(8,128)} %fusion.29), kind=kCustom, calls=%fused_computation.3.clone.1 | custom fusion | flops 2097152 | bytes 25165952 | tf_op jit(solution)/shard_map/while/body/scatter-add | solution.py:42
  159.8 0.7 add_compare_fusion.4
  160.5 0.1 compare_select_fusion.7
  160.6 6.1 gather_fusion
  166.7 7.0 fusion.29
  173.7 18.1 %scatter_fusion = f32[32,128,512]{2,1,0:T(8,128)} fusion(f32[32,128,512]{2,1,0:T(8,128)} %get-tuple-element.257, s32[32]{0:T(128)S(1)} %get-tuple-element.232, f32[32,128,512]{2,1,0:T(8,128)} %fusion.29), kind=kCustom, calls=%fused_computation.3.clone.1 | custom fusion | flops 2097152 | bytes 25165952 | tf_op jit(solution)/shard_map/while/body/scatter-add | solution.py:42
  191.8 0.0 all-reduce.3.cloned.1.call-update
  191.8 0.0 reduce-scatter.2.cloned.1.call-start
  191.9 8.6 copy.10
  200.5 275.5 %all-reduce.3.cloned.1.call-done = f32[4096,512]{1,0:T(8,128)} async-done(((f32[4096,512]{1,0:T(8,128)}), f32[4096,512]{1,0:T(8,128)}) %all-reduce.3.cloned.1.call-update) | async-done | bytes 8388624 | tf_op jit(solution)/shard_map/psum | solution.py:73
  476.0 7.6 multiply_convert_fusion
  483.7 7.9 broadcast_in_dim.38
  491.5 94.5 %while.21 = (s32[]{:T(128)}, f32[64,128,512]{2,1,0:T(8,128)}, s32[]{:T(128)}, s32[192]{0:T(256)S(1)}, s32[]{:T(128)}, /*index=5*/bf16[192,128,128]{1,2,0:T(8,128...) while((s32[]{:T(128)}, f32[64,128,512]{2,1,0:T(8,128)}, ...), condition=%wide.region_7.8_spmd, body=%wide.region_5.7_spmd.sunk | while | flops 539493632 | bytes 47191152 | solution.py:49
  491.5 0.7 add_compare_fusion.5
  492.2 0.1 compare_select_fusion.8
  492.3 5.1 gather_fusion.1
  497.4 7.0 fusion.32
  504.4 18.6 %scatter_fusion.1 = f32[64,128,512]{2,1,0:T(8,128)} fusion(f32[64,128,512]{2,1,0:T(8,128)} %get-tuple-element.293, s32[32]{0:T(128)S(1)} %get-tuple-element.242, f32[32,128,512]{2,1,0:T(8,128)} %fusion.32), kind=kCustom, calls=%fused_computation.4.clone.1 | custom fusion | flops 2097152 | bytes 25165952 | tf_op jit(solution)/shard_map/while/body/scatter-add | solution.py:47
  523.0 0.7 add_compare_fusion.5
  523.6 0.1 compare_select_fusion.8
  523.7 5.1 gather_fusion.1
  528.8 7.0 fusion.32
  535.8 18.6 %scatter_fusion.1 = f32[64,128,512]{2,1,0:T(8,128)} fusion(f32[64,128,512]{2,1,0:T(8,128)} %get-tuple-element.293, s32[32]{0:T(128)S(1)} %get-tuple-element.242, f32[32,128,512]{2,1,0:T(8,128)} %fusion.32), kind=kCustom, calls=%fused_computation.4.clone.1 | custom fusion | flops 2097152 | bytes 25165952 | tf_op jit(solution)/shard_map/while/body/scatter-add | solution.py:47
  554.4 0.7 add_compare_fusion.5
  555.1 0.1 compare_select_fusion.8
  555.2 5.1 gather_fusion.1
  560.3 7.0 fusion.32
  567.3 18.7 %scatter_fusion.1 = f32[64,128,512]{2,1,0:T(8,128)} fusion(f32[64,128,512]{2,1,0:T(8,128)} %get-tuple-element.293, s32[32]{0:T(128)S(1)} %get-tuple-element.242, f32[32,128,512]{2,1,0:T(8,128)} %fusion.32), kind=kCustom, calls=%fused_computation.4.clone.1 | custom fusion | flops 2097152 | bytes 25165952 | tf_op jit(solution)/shard_map/while/body/scatter-add | solution.py:47
  586.0 0.0 reduce-scatter.2.cloned.1.call-update
  586.1 0.0 all-reduce.5.cloned.1.call-start
  586.1 189.1 %reduce-scatter.2.cloned.1.call-done = f32[512,512]{1,0:T(8,128)} async-done(((f32[8192,512]{1,0:T(8,128)}), f32[512,512]{1,0:T(8,128)}) %reduce-scatter.2.cloned.1.call-update) | async-done | bytes 1048592 | tf_op jit(solution)/shard_map/reduce_scatter | solution.py:80
  775.2 3.3 fusion.14
  778.5 0.0 all-reduce.5.cloned.1.call-update
  778.5 2.3 multiply_convert_fusion.1
  780.8 147.3 %all-reduce.5.cloned.1.call-done = f32[512,512]{1,0:T(8,128)} async-done(((f32[512,512]{1,0:T(8,128)}), f32[512,512]{1,0:T(8,128)}) %all-reduce.5.cloned.1.call-update) | async-done | bytes 1048592 | tf_op jit(solution)/shard_map/psum | solution.py:87
  928.1 2.3 broadcast_multiply_fusion
  (14 shorter events, 0.1 us)
Async XLA Ops:
  7.2 4.6 copy-start
  7.2 83.3 %all-gather.2.cloned.1.call-start = ((), (), s32[]{:S(2)}) async-start(), calls=%async_computation.2 | async-start | bytes 8912896 | tf_op jit(solution)/shard_map/all_gather | solution.py:68
  11.7 83.0 %copy-start.4 = (s32[1,1,192]{2,1,0:T(1,128)S(1)}, s32[1,1,192]{2,1,0:T(1,128)}, u32[]{:S(2)}) copy-start(s32[1,1,192]{2,1,0:T(1,128)} %param.16) | copy-start | bytes 2308
  11.8 83.0 %copy-start.5 = (s32[1,1,192]{2,1,0:T(1,128)S(1)}, s32[1,1,192]{2,1,0:T(1,128)}, u32[]{:S(2)}) copy-start(s32[1,1,192]{2,1,0:T(1,128)} %param.17) | copy-start | bytes 2308
  37.9 56.9 %copy-start.2 = (bf16[512,512]{1,0:T(8,128)(2,1)}, bf16[512,512]{1,0:T(8,128)(2,1)S(1)}, u32[]{:S(2)}) copy-start(bf16[512,512]{1,0:T(8,128)(2,1)S(1)} %reshape.49) | copy-start | bytes 1572868
  40.4 435.7 %all-reduce.3.cloned.1.call-start = ((), (), s32[]{:S(2)}) async-start(), calls=%async_computation.3 | async-start | bytes 16777216 | tf_op jit(solution)/shard_map/psum | solution.py:73
  191.8 583.4 %reduce-scatter.2.cloned.1.call-start = ((), (), s32[]{:S(2)}) async-start(), calls=%async_computation.4 | async-start | bytes 17825792 | tf_op jit(solution)/shard_map/reduce_scatter | solution.py:80
  586.0 344.4 %copy-start.1 = (bf16[512,512]{1,0:T(8,128)(2,1)S(1)}, bf16[512,512]{1,0:T(8,128)(2,1)}, u32[]{:S(2)}) copy-start(bf16[512,512]{1,0:T(8,128)(2,1)} %param.12) | copy-start | bytes 1572868
  586.0 189.2 %copy-start.3 = (bf16[512,512]{1,0:T(8,128)(2,1)S(1)}, bf16[512,512]{1,0:T(8,128)(2,1)}, u32[]{:S(2)}) copy-start(bf16[512,512]{1,0:T(8,128)(2,1)} %copy-done.2) | copy-start | bytes 1572868
  586.1 342.1 %all-reduce.5.cloned.1.call-start = ((), (), s32[]{:S(2)}) async-start(), calls=%async_computation.5 | async-start | bytes 2097152 | tf_op jit(solution)/shard_map/psum | solution.py:87
Sparse Core Ops, SparseCore 0:
  40.5 49.9 all-gather.1
  192.0 284.0 all-reduce.2
  586.2 188.9 reduce-scatter.1
  780.4 147.6 all-reduce.4
where the time goes:
time: 939 us; the launch traced here: 937 us
  waiting for transfers between devices  661 us (70%)
  other arithmetic  132 us (14%)
  local copies, waits for them, and re-layouts  56.7 us (6%)
  matrix products  47.8 us (5%)
  blocking collectives  23.8 us (3%)
  between operations  14.5 us (2%)
    psum x1, waiting for transfers between devices, shards(): pre = lax.psum(partial_value, 'col')  276 us
    reduce_scatter x1, waiting for transfers between devices, shards(): lax.psum_scatter(back_partial, 'row', scatter_dimension=0, tiled=True)  189 us
    psum x1, waiting for transfers between devices, shards(): lax.psum(local_grad, ('row', 'col'))  147 us
    scatter-add x3, other arithmetic, one_block(): return totals.at[column_part].add(products)  55.9 us
    scatter-add x3, other arithmetic, one_block(): return totals.at[row_part].add(products)  55.4 us
    all_gather x1, waiting for transfers between devices, shards(): hidden_columns = lax.all_gather(hidden, 'row', axis=0, tiled=True)  49.4 us
    all_to_all x1, blocking collectives, regroup(): lax.all_to_all(shaped, ('row', 'col'), split_axis=0, concat_axis=0, tiled...  23.8 us
    dot_general x3, matrix products, one_block(): jnp.einsum('tij,tjf->tif', tile_block, picked, preferred_element_type=jnp...  21.1 us
  transfers between devices with their start and end apart: 4, of which 4 were waited for; matrix products, arithmetic and copies ran while one was open for 1% of the time, Pallas kernels for 0%

commit v1 on v0

--- a/solution.py
+++ b/solution.py
@@ -84,7 +84,9 @@
         precision=lax.Precision.HIGHEST,
         preferred_element_type=jnp.float32,
     )
-    weight_grad = lax.psum(local_grad, ("row", "col")) * (1.0 / math.sqrt(slots * n_row * n_col))
+    weight_grad = lax.psum(lax.psum(local_grad, "row"), "col") * (
+        1.0 / math.sqrt(slots * n_row * n_col)
+    )
     return (activations, weight_grad)
 
 

time: 939 us -> 999 us (1.064)
  waiting for transfers between devices: 661 us -> 718 us
    psum x1 -> x2, waiting for transfers between devices: 147 us -> 204 us  [the longest x1 120 us: shards(): lax.psum(local_grad, 'row')]
  transfers between devices with their start and end apart: 4 -> 5, of which waited for: 4 -> 5; matrix products, arithmetic and copies ran while one was open for 1% -> 1% of each run, Pallas kernels for 0% -> 0%
where the time goes in v1:
time: 999 us; the launch traced here: 993 us
  waiting for transfers between devices  718 us (72%)
  other arithmetic  132 us (13%)
  local copies, waits for them, and re-layouts  56.7 us (6%)
  matrix products  47.8 us (5%)
  blocking collectives  23.8 us (2%)
  between operations  14.5 us (1%)
    psum x1, waiting for transfers between devices, shards(): pre = lax.psum(partial_value, 'col')  276 us
    reduce_scatter x1, waiting for transfers between devices, shards(): lax.psum_scatter(back_partial, 'row', scatter_dimension=0, tiled=True)  189 us
    psum x1, waiting for transfers between devices, shards(): lax.psum(local_grad, 'row')  120 us
    psum x1, waiting for transfers between devices, shards(): lax.psum(lax.psum(local_grad, 'row'), 'col')  83.9 us
    scatter-add x3, other arithmetic, one_block(): return totals.at[column_part].add(products)  55.9 us
    scatter-add x3, other arithmetic, one_block(): return totals.at[row_part].add(products)  55.4 us
    all_gather x1, waiting for transfers between devices, shards(): hidden_columns = lax.all_gather(hidden, 'row', axis=0, tiled=True)  49.4 us
    all_to_all x1, blocking collectives, regroup(): lax.all_to_all(shaped, ('row', 'col'), split_axis=0, concat_axis=0, tiled...  23.8 us
  transfers between devices with their start and end apart: 5, of which 5 were waited for; matrix products, arithmetic and copies ran while one was open for 1% of the time, Pallas kernels for 0%

profile of v1, /device:TPU:1, one launch (start us, length us, event | category | flops | bytes accessed | tf_op | source)
XLA Modules:
  0.0 993.3 jit_solution(4999705312898185267)
XLA Ops:
  7.2 0.0 copy-start
  7.2 0.0 all-gather.2.cloned.1.call-start
  7.2 4.5 sort.17
  11.7 0.0 copy-start.4
  11.8 0.0 copy-start.5
  11.8 2.0 gather_fusion.2
  13.8 0.1 reshape.48
  13.9 23.8 %all_to_all.5 = bf16[128,4,512]{2,1,0:T(4,128)(2,1)S(1)} all-to-all(bf16[128,4,512]{2,1,0:T(4,128)(2,1)S(1)} %reshape.48), channel_id=1, replica_groups=mesh['row'=16,'col'=8] {'row','col'}, dimensions={0} | all-to-all | bytes 1048576 | tf_op jit(solution)/shard_map/all_to_all | solution.py:19
  37.7 0.1 reshape.49
  37.9 2.5 convolution_convert_fusion
  40.3 0.0 all-gather.2.cloned.1.call-update
  40.4 0.0 all-reduce.4.cloned.1.call-start
  41.1 49.4 %all-gather.2.cloned.1.call-done = bf16[8192,512]{1,0:T(8,128)(2,1)} async-done(((bf16[512,512]{1,0:T(8,128)(2,1)}), bf16[8192,512]{1,0:T(8,128)(2,1)}) %all-gather.2.cloned.1.call-update) | async-done | bytes 8388624 | tf_op jit(solution)/shard_map/all_gather | solution.py:68
  90.5 4.3 broadcast_in_dim.36
  94.8 97.0 %while.20 = (s32[]{:T(128)}, f32[32,128,512]{2,1,0:T(8,128)}, s32[]{:T(128)}, s32[192]{0:T(256)S(1)}, s32[]{:T(128)}, /*index=5*/bf16[192,128,128]{2,1,0:T(8,128...) while((s32[]{:T(128)}, f32[32,128,512]{2,1,0:T(8,128)}, ...), condition=%wide.region_3.4_spmd, body=%wide.region_1.3_spmd.sunk | while | flops 539493632 | bytes 47191152 | solution.py:49
  94.8 0.7 add_compare_fusion.4
  95.5 0.1 compare_select_fusion.7
  95.6 6.1 gather_fusion
  101.7 7.0 fusion.29
  108.7 18.8 %scatter_fusion = f32[32,128,512]{2,1,0:T(8,128)} fusion(f32[32,128,512]{2,1,0:T(8,128)} %get-tuple-element.257, s32[32]{0:T(128)S(1)} %get-tuple-element.232, f32[32,128,512]{2,1,0:T(8,128)} %fusion.29), kind=kCustom, calls=%fused_computation.3.clone.1 | custom fusion | flops 2097152 | bytes 25165952 | tf_op jit(solution)/shard_map/while/body/scatter-add | solution.py:42
  127.5 0.7 add_compare_fusion.4
  128.2 0.1 compare_select_fusion.7
  128.3 6.1 gather_fusion
  134.4 7.0 fusion.29
  141.4 18.5 %scatter_fusion = f32[32,128,512]{2,1,0:T(8,128)} fusion(f32[32,128,512]{2,1,0:T(8,128)} %get-tuple-element.257, s32[32]{0:T(128)S(1)} %get-tuple-element.232, f32[32,128,512]{2,1,0:T(8,128)} %fusion.29), kind=kCustom, calls=%fused_computation.3.clone.1 | custom fusion | flops 2097152 | bytes 25165952 | tf_op jit(solution)/shard_map/while/body/scatter-add | solution.py:42
  159.8 0.7 add_compare_fusion.4
  160.5 0.1 compare_select_fusion.7
  160.6 6.1 gather_fusion
  166.7 7.0 fusion.29
  173.7 18.1 %scatter_fusion = f32[32,128,512]{2,1,0:T(8,128)} fusion(f32[32,128,512]{2,1,0:T(8,128)} %get-tuple-element.257, s32[32]{0:T(128)S(1)} %get-tuple-element.232, f32[32,128,512]{2,1,0:T(8,128)} %fusion.29), kind=kCustom, calls=%fused_computation.3.clone.1 | custom fusion | flops 2097152 | bytes 25165952 | tf_op jit(solution)/shard_map/while/body/scatter-add | solution.py:42
  191.8 0.0 all-reduce.4.cloned.1.call-update
  191.8 0.0 reduce-scatter.2.cloned.1.call-start
  191.9 8.6 copy.10
  200.5 275.5 %all-reduce.4.cloned.1.call-done = f32[4096,512]{1,0:T(8,128)} async-done(((f32[4096,512]{1,0:T(8,128)}), f32[4096,512]{1,0:T(8,128)}) %all-reduce.4.cloned.1.call-update) | async-done | bytes 8388624 | tf_op jit(solution)/shard_map/psum | solution.py:73
  476.0 7.6 multiply_convert_fusion
  483.7 7.9 broadcast_in_dim.38
  491.5 94.5 %while.21 = (s32[]{:T(128)}, f32[64,128,512]{2,1,0:T(8,128)}, s32[]{:T(128)}, s32[192]{0:T(256)S(1)}, s32[]{:T(128)}, /*index=5*/bf16[192,128,128]{1,2,0:T(8,128...) while((s32[]{:T(128)}, f32[64,128,512]{2,1,0:T(8,128)}, ...), condition=%wide.region_7.8_spmd, body=%wide.region_5.7_spmd.sunk | while | flops 539493632 | bytes 47191152 | solution.py:49
  491.5 0.7 add_compare_fusion.5
  492.2 0.1 compare_select_fusion.8
  492.3 5.1 gather_fusion.1
  497.4 7.0 fusion.32
  504.4 18.6 %scatter_fusion.1 = f32[64,128,512]{2,1,0:T(8,128)} fusion(f32[64,128,512]{2,1,0:T(8,128)} %get-tuple-element.293, s32[32]{0:T(128)S(1)} %get-tuple-element.242, f32[32,128,512]{2,1,0:T(8,128)} %fusion.32), kind=kCustom, calls=%fused_computation.4.clone.1 | custom fusion | flops 2097152 | bytes 25165952 | tf_op jit(solution)/shard_map/while/body/scatter-add | solution.py:47
  523.0 0.7 add_compare_fusion.5
  523.6 0.1 compare_select_fusion.8
  523.7 5.1 gather_fusion.1
  528.8 7.0 fusion.32
  535.8 18.6 %scatter_fusion.1 = f32[64,128,512]{2,1,0:T(8,128)} fusion(f32[64,128,512]{2,1,0:T(8,128)} %get-tuple-element.293, s32[32]{0:T(128)S(1)} %get-tuple-element.242, f32[32,128,512]{2,1,0:T(8,128)} %fusion.32), kind=kCustom, calls=%fused_computation.4.clone.1 | custom fusion | flops 2097152 | bytes 25165952 | tf_op jit(solution)/shard_map/while/body/scatter-add | solution.py:47
  554.4 0.7 add_compare_fusion.5
  555.1 0.1 compare_select_fusion.8
  555.2 5.1 gather_fusion.1
  560.3 7.0 fusion.32
  567.3 18.7 %scatter_fusion.1 = f32[64,128,512]{2,1,0:T(8,128)} fusion(f32[64,128,512]{2,1,0:T(8,128)} %get-tuple-element.293, s32[32]{0:T(128)S(1)} %get-tuple-element.242, f32[32,128,512]{2,1,0:T(8,128)} %fusion.32), kind=kCustom, calls=%fused_computation.4.clone.1 | custom fusion | flops 2097152 | bytes 25165952 | tf_op jit(solution)/shard_map/while/body/scatter-add | solution.py:47
  586.0 0.0 reduce-scatter.2.cloned.1.call-update
  586.1 0.0 copy-start.1
  586.1 0.0 all-reduce.6.cloned.1.call-start
  586.1 189.1 %reduce-scatter.2.cloned.1.call-done = f32[512,512]{1,0:T(8,128)} async-done(((f32[8192,512]{1,0:T(8,128)}), f32[512,512]{1,0:T(8,128)}) %reduce-scatter.2.cloned.1.call-update) | async-done | bytes 1048592 | tf_op jit(solution)/shard_map/reduce_scatter | solution.py:80
  775.2 3.3 fusion.14
  778.5 0.0 all-reduce.6.cloned.1.call-update
  778.5 0.0 all-reduce.8.cloned.1.call-start
  778.6 119.7 %all-reduce.6.cloned.1.call-done = f32[512,512]{1,0:T(8,128)} async-done(((f32[512,512]{1,0:T(8,128)}), f32[512,512]{1,0:T(8,128)}) %all-reduce.6.cloned.1.call-update) | async-done | bytes 1048592 | tf_op jit(solution)/shard_map/psum | solution.py:87
  898.3 0.0 all-reduce.8.cloned.1.call-update
  898.3 2.3 multiply_convert_fusion.1
  900.6 83.9 %all-reduce.8.cloned.1.call-done = f32[512,512]{1,0:T(8,128)} async-done(((f32[512,512]{1,0:T(8,128)}), f32[512,512]{1,0:T(8,128)}) %all-reduce.8.cloned.1.call-update) | async-done | bytes 1048592 | tf_op jit(solution)/shard_map/psum | solution.py:87
  984.5 2.3 broadcast_multiply_fusion
  (17 shorter events, 0.1 us)
Async XLA Ops:
  7.2 4.6 copy-start
  7.2 83.3 %all-gather.2.cloned.1.call-start = ((), (), s32[]{:S(2)}) async-start(), calls=%async_computation.2 | async-start | bytes 8912896 | tf_op jit(solution)/shard_map/all_gather | solution.py:68
  11.7 83.0 %copy-start.4 = (s32[1,1,192]{2,1,0:T(1,128)S(1)}, s32[1,1,192]{2,1,0:T(1,128)}, u32[]{:S(2)}) copy-start(s32[1,1,192]{2,1,0:T(1,128)} %param.16) | copy-start | bytes 2308
  11.8 83.0 %copy-start.5 = (s32[1,1,192]{2,1,0:T(1,128)S(1)}, s32[1,1,192]{2,1,0:T(1,128)}, u32[]{:S(2)}) copy-start(s32[1,1,192]{2,1,0:T(1,128)} %param.17) | copy-start | bytes 2308
  37.9 56.9 %copy-start.2 = (bf16[512,512]{1,0:T(8,128)(2,1)}, bf16[512,512]{1,0:T(8,128)(2,1)S(1)}, u32[]{:S(2)}) copy-start(bf16[512,512]{1,0:T(8,128)(2,1)S(1)} %reshape.49) | copy-start | bytes 1572868
  40.4 435.7 %all-reduce.4.cloned.1.call-start = ((), (), s32[]{:S(2)}) async-start(), calls=%async_computation.3 | async-start | bytes 16777216 | tf_op jit(solution)/shard_map/psum | solution.py:73
  191.8 583.4 %reduce-scatter.2.cloned.1.call-start = ((), (), s32[]{:S(2)}) async-start(), calls=%async_computation.4 | async-start | bytes 17825792 | tf_op jit(solution)/shard_map/reduce_scatter | solution.py:80
  586.0 189.2 %copy-start.3 = (bf16[512,512]{1,0:T(8,128)(2,1)S(1)}, bf16[512,512]{1,0:T(8,128)(2,1)}, u32[]{:S(2)}) copy-start(bf16[512,512]{1,0:T(8,128)(2,1)} %copy-done.2) | copy-start | bytes 1572868
  586.1 400.7 %copy-start.1 = (bf16[512,512]{1,0:T(8,128)(2,1)S(1)}, bf16[512,512]{1,0:T(8,128)(2,1)}, u32[]{:S(2)}) copy-start(bf16[512,512]{1,0:T(8,128)(2,1)} %param.12) | copy-start | bytes 1572868
  586.1 312.2 %all-reduce.6.cloned.1.call-start = ((), (), s32[]{:S(2)}) async-start(), calls=%async_computation.5 | async-start | bytes 2097152 | tf_op jit(solution)/shard_map/psum | solution.py:87
  778.5 206.0 %all-reduce.8.cloned.1.call-start = ((), (), s32[]{:S(2)}) async-start(), calls=%async_computation.6 | async-start | bytes 2097152 | tf_op jit(solution)/shard_map/psum | solution.py:87
Sparse Core Ops, SparseCore 0:
  40.5 49.9 all-gather.1
  192.0 284.0 all-reduce.3
  586.2 188.9 reduce-scatter.1
  778.6 119.5 all-reduce.5
  900.8 83.6 all-reduce.7
